TPU v7x, 32 devices: a whole 2x2x4 slice. The times are simulated.
32 devices in a mesh: wide: 8 (over z, core), narrow: 4 (over y, x).
Axes of the slice: x: 2, y: 2, z: 4, core: 2. Of those that a mesh axis runs over, the one named last changes fastest.
Arguments:
- rhs_panels: float32 [2, 1024, 4096], P(None, 'narrow', 'wide'), may hold values from -6 to 6
- rhs_rest: float32 [12288, 4096], P('narrow', 'wide'), may hold values from -6 to 6
- diag_inv: float32 [8, 1024, 1024], P('wide', 'narrow'), as said below
- couple: float32 [8, 1024, 1024], P('wide', 'narrow'), may hold values from -0.1875 to 0.1875
- off_blocks: float32 [8, 6144, 1024], P('wide', 'narrow'), may hold values from -0.1875 to 0.1875
- pattern: int32 [2, 24], P(None, 'narrow'), may hold values from 0 to 47, as said below
- owner: int32 [2], replicated, may hold values from 0 to 7, as said below
Outputs:
- solved: float32 [2, 1024, 4096], P(None, 'narrow', 'wide')
- rest_out: float32 [12288, 4096], P('narrow', 'wide')
Inputs may be any that keep to these rules, and one draw needn't show every extreme that they name: `pattern`: entries j * 6 to (j + 1) * 6 - 1 of each row are 6 different increasing block numbers among j * 12 to (j + 1) * 12 - 1. `owner`: two different slots, one of them slot 7. `diag_inv`: each slot is lower triangular with a nonzero diagonal.
All inputs are finite; a program needn't handle non-finite values.
Results may differ from a plain program's by a relative error of at most 0.00012.
Values sent between devices are 32-bit elements; how exact they have to be, the bound alone decides.
A program may use at most 128 MiB of HBM per device.

v0:
```python
import jax
import jax.numpy as jnp
from jax import lax
from jax.sharding import PartitionSpec as P

BLK = 256


def from_root(block, axis, owner):
    block = jnp.where(lax.axis_index(axis) == owner, block, jnp.zeros_like(block))
    return lax.psum(block, axis)


def matmul(left, right):
    return jnp.dot(left, right, preferred_element_type=jnp.float32, precision=lax.Precision.HIGHEST)


def solve_panel(inverse_rows, rows_here):
    full_rhs = lax.all_gather(rows_here, "narrow", axis=0, tiled=True)
    own_rows = matmul(inverse_rows, full_rhs)
    whole_solved = lax.all_gather(own_rows, "narrow", axis=0, tiled=True)
    return (own_rows, whole_solved)


def apply_panel(remainder, off_rows, unknowns, indices):
    width = remainder.shape[1]
    blocks_here = remainder.shape[0] // BLK
    updates = matmul(off_rows, unknowns).reshape(-1, BLK, width)
    local_block = indices - lax.axis_index("narrow") * blocks_here
    select = (local_block[:, None] == jnp.arange(blocks_here, dtype=jnp.int32)[None, :]).astype(
        jnp.float32
    )
    change = jnp.einsum("ob,orc->brc", select, updates, precision=lax.Precision.HIGHEST)
    return remainder - change.reshape(remainder.shape)


def per_device(rhs_panels, rhs_rest, diag_inv, couple, off_blocks, pattern, owner):
    first_data = (
        from_root(diag_inv[0], "wide", owner[0]),
        from_root(couple[0], "wide", owner[0]),
        from_root(off_blocks[0], "wide", owner[0]),
    )
    second_data = (
        from_root(diag_inv[0], "wide", owner[1]),
        from_root(off_blocks[0], "wide", owner[1]),
    )
    first_own, first_whole = solve_panel(first_data[0], rhs_panels[0])
    second_rhs = rhs_panels[1] - matmul(first_data[1], first_whole)
    second_own, second_whole = solve_panel(second_data[0], second_rhs)
    remainder = apply_panel(rhs_rest, first_data[2], first_whole, pattern[0])
    remainder = apply_panel(remainder, second_data[1], second_whole, pattern[1])
    return (jnp.stack([first_own, second_own]), remainder)


def solution(mesh):
    in_specs = (
        P(None, "narrow", "wide"),
        P("narrow", "wide"),
        P("wide", "narrow", None),
        P("wide", "narrow", None),
        P("wide", "narrow", None),
        P(None, "narrow"),
        P(),
    )
    out_specs = (P(None, "narrow", "wide"), P("narrow", "wide"))
    return jax.shard_map(
        per_device, mesh=mesh, in_specs=in_specs, out_specs=out_specs, check_vma=False
    )
```

profile of v0, /device:TPU:0, one launch (start us, length us, event | category | flops | bytes accessed | tf_op | source)
XLA Modules:
  0.0 513.2 jit_solution(4029680594437295367)
XLA Ops:
  8.0 1.9 slice.22
  9.9 0.0 all-reduce.3.cloned.1.call-start
  10.0 1.3 fusion.12
  12.6 3.0 select_bitcast_fusion.4
  15.6 9.8 %select_bitcast_fusion.1 = (f32[1536,1024]{1,0:T(8,128)}, f32[1536,1024]{1,0:T(8,128)}) fusion(f32[1,1536,1024]{2,1,0:T(8,128)} %param.11, pred[]{:T(512)S(6)} %eq.16, pred[]{:T(512)S(6)} %eq.17), kind=kLoop, calls=%fused_computation.3 | loop fusion | flops 3145728 | bytes 18874370 | tf_op jit(solution)/shard_map/jit(_where)/select_n | solution.py:10
  25.4 0.0 all-gather.6.cloned.1.call-start
  25.5 23.3 %all-gather.12.cloned.1.call-done = f32[1,1024,512]{2,1,0:T(8,128)} async-done(((f32[1,256,512]{2,1,0:T(8,128)}), f32[1,1024,512]{2,1,0:T(8,128)}) %all-gather.12.cloned.1.call-update) | async-done | bytes 2097168 | tf_op jit(solution)/shard_map/all_gather | solution.py:19
  48.7 294.6 %all-reduce.3.cloned.1.call-done = (f32[256,1024]{1,0:T(8,128)}, f32[256,1024]{1,0:T(8,128)}, f32[256,1024]{1,0:T(8,128)}, f32[1536,1024]{1,0:T(8,128)}, f32[1536,1024]{1,0:T(8,128)}) async-done(((f32[256,1024]{1,0:T(8,128)}, f32[256,1024]{1,0:T(8,128)}, f32[256,1024]{1,0:T(8,128)}, f32[1536,1024]{1,0:T(8,128)}, f32[1536,1024]{1,0:T(8,128)}), (f32[256,1024]{1,0:T(8,128)}, f32[256,1024]{1,0:T(8,128)}, ...) | async-done | bytes 15728656 | tf_op jit(solution)/shard_map/psum | solution.py:11
  343.3 4.7 fusion.4
  348.1 0.0 all-gather.8.cloned.1.call-start
  348.1 35.6 %all-gather.6.cloned.1.call-done = f32[1024,512]{1,0:T(8,128)} async-done(((f32[256,512]{1,0:T(8,128)}), f32[1024,512]{1,0:T(8,128)}) %all-gather.6.cloned.1.call-update) | async-done | bytes 2097168 | tf_op jit(solution)/shard_map/all_gather | solution.py:21
  383.8 4.9 convolution_subtract_fusion
  388.7 0.0 all-gather.10.cloned.1.call-start
  388.7 35.4 %all-gather.8.cloned.1.call-done = f32[1024,512]{1,0:T(8,128)} async-done(((f32[256,512]{1,0:T(8,128)}), f32[1024,512]{1,0:T(8,128)}) %all-gather.8.cloned.1.call-update) | async-done | bytes 2097168 | tf_op jit(solution)/shard_map/all_gather | solution.py:19
  424.1 4.3 fusion.13
  428.5 12.3 %fusion.14 = f32[1536,512]{1,0:T(8,128)S(1)} fusion(f32[1536,1024]{1,0:T(8,128)} %get-tuple-element.6, f32[1024,512]{1,0:T(8,128)S(1)} %copy-done), kind=kOutput, calls=%fused_computation.25 | convolution fusion | flops 9663676416 | bytes 11534336 | tf_op jit(solution)/shard_map/dot_general | solution.py:15
  440.8 5.3 %fusion.2 = f32[12,256,512]{2,0,1:T(8,128)S(1)} fusion(f32[6,256,512]{2,1,0:T(8,128)S(1)} %bitcast.47, s32[6]{0:T(128)S(1)} %get-tuple-element.11), kind=kOutput, calls=%fused_computation.6 | convolution fusion | flops 113246280 | bytes 9437208 | tf_op jit(solution)/shard_map/ob,orc->brc/dot_general | solution.py:33
  446.2 6.3 %copy.12 = f32[12,256,512]{2,1,0:T(8,128)} copy(f32[12,256,512]{2,0,1:T(8,128)S(1)} %fusion.2) | data formatting | bytes 12582912 | tf_op jit(solution)/shard_map/ob,orc->brc/dot_general | solution.py:33
  452.5 1.0 pad_maximum_fusion
  453.6 10.4 %all-gather.10.cloned.1.call-done = f32[1024,512]{1,0:T(8,128)} async-done(((f32[256,512]{1,0:T(8,128)}), f32[1024,512]{1,0:T(8,128)}) %all-gather.10.cloned.1.call-update) | async-done | bytes 2097168 | tf_op jit(solution)/shard_map/all_gather | solution.py:21
  464.0 21.4 %fusion.15 = f32[1536,512]{1,0:T(8,128)S(1)} fusion(f32[1536,1024]{1,0:T(8,128)} %get-tuple-element.5, f32[1024,512]{1,0:T(8,128)} %all-gather.10.cloned.1.call-done), kind=kOutput, calls=%fused_computation.26 | convolution fusion | flops 9663676416 | bytes 11534336 | tf_op jit(solution)/shard_map/dot_general | solution.py:15
  485.3 5.3 %fusion = f32[12,256,512]{2,0,1:T(8,128)S(1)} fusion(f32[6,256,512]{2,1,0:T(8,128)S(1)} %bitcast.46, s32[6]{0:T(128)S(1)} %get-tuple-element.12), kind=kOutput, calls=%fused_computation.4 | convolution fusion | flops 113246280 | bytes 9437208 | tf_op jit(solution)/shard_map/ob,orc->brc/dot_general | solution.py:33
  490.7 6.3 %copy.14 = f32[12,256,512]{2,1,0:T(8,128)} copy(f32[12,256,512]{2,0,1:T(8,128)S(1)} %fusion) | data formatting | bytes 12582912 | tf_op jit(solution)/shard_map/ob,orc->brc/dot_general | solution.py:33
  496.9 8.9 %bitcast_subtract_fusion = f32[3072,512]{1,0:T(8,128)} fusion(f32[12,256,512]{2,1,0:T(8,128)} %copy.14, f32[3072,512]{1,0:T(8,128)} %param.8, f32[12,256,512]{2,1,0:T(8,128)S(1)} %bitcast.49), kind=kLoop, calls=%fused_computation | loop fusion | flops 3145728 | bytes 25165824 | tf_op jit(solution)/shard_map/sub | solution.py:34
  (22 shorter events, 0.2 us)
Async XLA Ops:
  8.0 40.7 %all-gather.12.cloned.1.call-start = ((), (), s32[]{:S(2)}) async-start(), calls=%async_computation.3 | async-start | bytes 2621440 | tf_op jit(solution)/shard_map/all_gather | solution.py:19
  9.9 333.4 %all-reduce.3.cloned.1.call-start = ((), (), s32[]{:S(2)}) async-start(), calls=%async_computation.4 | async-start | bytes 31457280 | tf_op jit(solution)/shard_map/psum | solution.py:11
  25.4 358.4 %all-gather.6.cloned.1.call-start = ((), (), s32[]{:S(2)}) async-start(), calls=%async_computation | async-start | bytes 2621440 | tf_op jit(solution)/shard_map/all_gather | solution.py:21
  343.3 80.8 %copy-start.3 = (f32[256,1024]{1,0:T(8,128)S(1)}, f32[256,1024]{1,0:T(8,128)}, u32[]{:S(2)}) copy-start(f32[256,1024]{1,0:T(8,128)} %get-tuple-element.2) | copy-start | bytes 3145732
  348.1 76.1 %all-gather.8.cloned.1.call-start = ((), (), s32[]{:S(2)}) async-start(), calls=%async_computation.1 | async-start | bytes 2621440 | tf_op jit(solution)/shard_map/all_gather | solution.py:19
  383.8 44.7 %copy-start.4 = (s32[2,6]{1,0:T(2,128)S(1)}, s32[2,6]{1,0:T(2,128)}, u32[]{:S(2)}) copy-start(s32[2,6]{1,0:T(2,128)} %param.12) | copy-start | bytes 148
  383.8 44.7 %copy-start = (f32[1024,512]{1,0:T(8,128)S(1)}, f32[1024,512]{1,0:T(8,128)}, u32[]{:S(2)}) copy-start(f32[1024,512]{1,0:T(8,128)} %all-gather.6.cloned.1.call-done) | copy-start | bytes 6291460
  388.7 75.3 %all-gather.10.cloned.1.call-start = ((), (), s32[]{:S(2)}) async-start(), calls=%async_computation.2 | async-start | bytes 2621440 | tf_op jit(solution)/shard_map/all_gather | solution.py:21
  446.2 6.4 %copy-start.1 = (f32[256,512]{1,0:T(8,128)S(1)}, f32[256,512]{1,0:T(8,128)}, u32[]{:S(2)}) copy-start(f32[256,512]{1,0:T(8,128)} %fusion.4) | copy-start | bytes 1572868
  446.2 6.4 %copy-start.2 = (f32[256,512]{1,0:T(8,128)S(1)}, f32[256,512]{1,0:T(8,128)}, u32[]{:S(2)}) copy-start(f32[256,512]{1,0:T(8,128)} %fusion.13) | copy-start | bytes 1572868
  485.3 11.6 %slice-start = ((s8[6291456]{0:T(1024)(128)(4,1)}), s8[4194304]{0:T(1024)(128)(4,1)S(1)}, s32[]{:S(2)}) async-start(s8[6291456]{0:T(1024)(128)(4,1)} %bitcast.48), calls=%async_computation.5 | async-start | bytes 8388608
  490.6 6.3 %slice-start.1 = ((s8[6291456]{0:T(1024)(128)(4,1)}), s8[2097152]{0:T(1024)(128)(4,1)S(1)}, s32[]{:S(2)}) async-start(s8[6291456]{0:T(1024)(128)(4,1)} %bitcast.48), calls=%async_computation.6 | async-start | bytes 4194304
Sparse Core Ops, SparseCore 0:
  10.7 38.0 all-gather.11
  348.2 35.5 all-gather.5
  388.8 35.2 all-gather.7
  428.6 35.2 all-gather.9
Sparse Core Ops, SparseCore 1:
  25.5 317.8 all-reduce.2
where the time goes:
time: 517 us; the launch traced here: 513 us
  waiting for transfers between devices  399 us (77%)
  matrix products  58.2 us (11%)
  other arithmetic  22.7 us (4%)
  between operations  16.8 us (3%)
  local copies, waits for them, and re-layouts  15.9 us (3%)
    psum x1, waiting for transfers between devices, from_root(): return lax.psum(block, axis)  295 us
    all_gather x2, waiting for transfers between devices, solve_panel(): full_rhs = lax.all_gather(rows_here, 'narrow', axis=0, tiled=True)  58.7 us
    dot_general x5, matrix products, matmul(): jnp.dot(left, right, preferred_element_type=jnp.float32, precision=lax.Pr...  47.6 us
    all_gather x2, waiting for transfers between devices, solve_panel(): whole_solved = lax.all_gather(own_rows, 'narrow', axis=0, tiled=True)  46 us
    select_n x2, other arithmetic, from_root(): jnp.where(lax.axis_index(axis) == owner, block, jnp.zeros_like(block))  12.8 us
    dot_general x2, local copies, waits for them, and re-layouts, apply_panel(): jnp.einsum('ob,orc->brc', select, updates, precision=lax.Precision.HIGHEST)  12.6 us
    dot_general x2, matrix products, apply_panel(): jnp.einsum('ob,orc->brc', select, updates, precision=lax.Precision.HIGHEST)  10.6 us
  transfers between devices with their start and end apart: 5, of which 5 were waited for; matrix products, arithmetic and copies ran while one was open for 8% of the time, Pallas kernels for 0%

commit v1 on v0

v1 whole, which is shorter than its diff:
```python
import functools

import jax
import jax.numpy as jnp
from jax import lax
from jax.experimental import pallas as pl
from jax.experimental.pallas import tpu as pltpu
from jax.sharding import PartitionSpec as P

BLK = 256
CH = 32
SKEW = 2
GROUP = 4
GAP = 10


def split(value):
    high = value.astype(jnp.bfloat16)
    low = (value - high.astype(jnp.float32)).astype(jnp.bfloat16)
    return high, low


def dot3(left, high, low):
    left_high, left_low = split(left)
    dot = functools.partial(jnp.dot, preferred_element_type=jnp.float32)
    return dot(left_high, high) + (dot(left_high, low) + dot(left_low, high))


def panels_kernel(
    pairs, narrow, owner_ref, rhs_ref, diag_ref, couple_ref, off_ref, solved_ref, u_ref,
    mine, sib, up, dn, other, full, xh, xl,
    load_sem, sib_send, sib_recv, up_send, up_recv, dn_send, dn_recv,
    pair_send, pair_recv, row_send, row_recv,
):
    wide = lax.axis_index("wide")
    row = lax.axis_index("narrow")
    pair = wide // 2
    half = wide % 2
    rows = diag_ref.shape[1]
    off_rows = off_ref.shape[1]
    depth = diag_ref.shape[2]
    part = rows // 2
    off_part = off_rows // 2
    nd = part // CH
    no = off_part // CH
    chunks = 3 * nd + 2 * no
    groups = no // GROUP

    def at(w, r):
        return dict(device_id=(w, r), device_id_type=pl.DeviceIdType.MESH)

    sibling = wide + 1 - 2 * half
    barrier = pltpu.get_barrier_semaphore()
    pl.semaphore_signal(barrier, inc=1, **at(sibling, row))
    for d in range(1, narrow):
        pl.semaphore_signal(barrier, inc=1, **at(wide, (row + d) % narrow))

    @pl.when(pair > 0)
    def _():
        pl.semaphore_signal(barrier, inc=1, **at(wide - 2, row))

    @pl.when(pair < pairs - 1)
    def _():
        pl.semaphore_signal(barrier, inc=1, **at(wide + 2, row))

    sources = ((diag_ref, 0, part), (couple_ref, part, part), (off_ref, 2 * part, off_part))

    def load(i):
        ref, base, size = sources[i]
        return pltpu.make_async_copy(
            ref.at[0, pl.ds(half * size, size)], mine.at[pl.ds(base, size)], load_sem.at[i]
        )

    def give(i):
        ref, base, size = sources[i]
        return pltpu.make_async_remote_copy(
            src_ref=ref.at[0, pl.ds((1 - half) * size, size)],
            dst_ref=sib.at[pl.ds(base, size)],
            send_sem=sib_send.at[i], recv_sem=sib_recv.at[i], **at(sibling, row),
        )

    for i in range(3):
        load(i).start()
    inner = (pair > 0) & (pair < pairs - 1)

    @pl.when(inner)
    def _():
        pl.semaphore_wait(barrier, narrow + 2)

    @pl.when(jnp.logical_not(inner))
    def _():
        pl.semaphore_wait(barrier, narrow + 1)

    for i in range(3):
        give(i).start()

    def gather(stage, d):
        here = full.at[stage, pl.ds(row * rows, rows)]
        return pltpu.make_async_remote_copy(
            src_ref=here, dst_ref=here,
            send_sem=row_send.at[stage, d - 1], recv_sem=row_recv.at[stage, d - 1],
            **at(wide, (row + d) % narrow),
        )

    def send_rows(stage, value):
        full[stage, pl.ds(row * rows, rows)] = value
        for d in range(1, narrow):
            gather(stage, d).start()

    def gathered(stage, slot):
        for d in range(1, narrow):
            came = full.at[stage, pl.ds((row + narrow - d) % narrow * rows, rows)]
            pltpu.make_async_remote_copy(
                src_ref=came, dst_ref=came,
                send_sem=row_send.at[stage, d - 1], recv_sem=row_recv.at[stage, d - 1],
                **at(wide, (row + d) % narrow),
            ).wait_recv()
        for d in range(1, narrow):
            gather(stage, d).wait_send()
        high, low = split(full[stage])
        xh[slot] = high
        xl[slot] = low

    send_rows(0, rhs_ref[0])
    for i in range(2):
        load(i).wait()
        give(i).wait()

    def mask(scalar):
        return jnp.full((CH, depth), scalar, jnp.int32) == 0

    segments = (
        (0, 0, nd, 0),
        (0, nd, nd, part),
        (1, 2 * nd, nd, 0),
        (0, 3 * nd, no, 2 * part),
        (1, 3 * nd + no, no, 2 * part),
    )

    def hop(k, step, buf, send_sem, recv_sem):
        return pltpu.make_async_remote_copy(
            src_ref=buf.at[k], dst_ref=buf.at[k],
            send_sem=send_sem.at[k], recv_sem=recv_sem.at[k], **at(wide + 2 * step, row),
        )

    def relay(k, step, buf, send_sem, recv_sem, has_in, has_out):
        for stream, start, count, base in segments:

            @pl.when((k >= start) & (k < start + count))
            def _():
                held = owner_ref[stream]
                window = pl.ds(base + (k - start) * CH, CH)

                @pl.when(has_in)
                def _():
                    hop(k, step, buf, send_sem, recv_sem).wait_recv()
                    value = jnp.where(mask(held - sibling), sib[window], buf[k])
                    buf[k] = jnp.where(mask(held - wide), mine[window], value)

                @pl.when(jnp.logical_not(has_in))
                def _():
                    buf[k] = jnp.where(mask(held - wide), mine[window], sib[window])

                @pl.when(has_out)
                def _():
                    hop(k, step, buf, send_sem, recv_sem).start()

    def share(k):
        return pltpu.make_async_remote_copy(
            src_ref=dn.at[k], dst_ref=other.at[k],
            send_sem=pair_send.at[k], recv_sem=pair_recv.at[k], **at(sibling, row),
        )

    def finish(k):
        @pl.when(pair < pairs - 1)
        def _():
            hop(k, 1, up, up_send, up_recv).wait_send()

        @pl.when(pair > 0)
        def _():
            hop(k, -1, dn, dn_send, dn_recv).wait_send()

        for stream, start, count, _base in segments:

            @pl.when((k >= start) & (k < start + count))
            def _():
                above = jnp.full((CH, depth), owner_ref[stream] // 2 - pair, jnp.int32) > 0
                dn[k] = jnp.where(above, dn[k], up[k])
                share(k).start()

    def landed(first, count):
        def wait(i, carry):
            share(first + i).wait()
            return carry

        lax.fori_loop(0, count, wait, 0)

    def rows_of(first, slot):
        landed(first, nd)
        own = dot3(dn[pl.ds(first, nd)].reshape(part, depth), xh[slot], xl[slot])
        far = dot3(other[pl.ds(first, nd)].reshape(part, depth), xh[slot], xl[slot])
        return own, far

    def put(ref, own, far):
        ref[pl.ds(half * part, part)] = own
        ref[pl.ds((1 - half) * part, part)] = far

    def update(stream, group):
        first = 3 * nd + stream * no + group * GROUP
        size = GROUP * CH
        landed(first, GROUP)
        own = dot3(dn[pl.ds(first, GROUP)].reshape(size, depth), xh[stream], xl[stream])
        u_ref[stream, pl.ds(half * off_part + group * size, size)] = own
        far = dot3(other[pl.ds(first, GROUP)].reshape(size, depth), xh[stream], xl[stream])
        u_ref[stream, pl.ds((1 - half) * off_part + group * size, size)] = far

    lag = SKEW * pairs
    first_at = max(3 * nd + GROUP, nd + GAP + 1)
    second_at = 3 * nd + no + GROUP

    def body(t, carry):
        @pl.when(t == 3 * nd)
        def _():
            load(2).wait()
            give(2).wait()

        relay(t - SKEW * pair, 1, up, up_send, up_recv, pair > 0, pair < pairs - 1)
        relay(
            t - SKEW * (pairs - 1 - pair), -1, dn, dn_send, dn_recv, pair < pairs - 1, pair > 0
        )
        f = t - lag

        @pl.when((f >= 0) & (f < chunks))
        def _():
            finish(f)

        @pl.when(f == nd)
        def _():
            gathered(0, 1)
            put(solved_ref.at[0], *rows_of(0, 1))
            send_rows(1, solved_ref[0])

        @pl.when(f == nd + GAP)
        def _():
            gathered(1, 0)
            put(solved_ref.at[1], *rows_of(nd, 0))
            send_rows(2, rhs_ref[1] - solved_ref[1])

        @pl.when(f == nd + 2 * GAP)
        def _():
            gathered(2, 1)
            put(solved_ref.at[1], *rows_of(2 * nd, 1))
            send_rows(3, solved_ref[1])

        g = f - first_at

        @pl.when((g >= 0) & (g < no) & (g % GROUP == 0))
        def _():
            update(0, g // GROUP)

        @pl.when(f == second_at)
        def _():
            gathered(3, 1)

        s = f - second_at

        @pl.when((s >= 0) & (s < no) & (s % GROUP == 0))
        def _():
            update(1, s // GROUP)

        return carry

    lax.fori_loop(0, lag + chunks + 1, body, 0)


def subtract_kernel(pattern_ref, rest_ref, first_ref, second_ref, out_ref):
    b = pl.program_id(0)
    count = pattern_ref.shape[1]
    total = rest_ref[...]
    for stream, ref in enumerate((first_ref, second_ref)):
        found = jnp.int32(0)
        for o in range(count):
            found = found + jnp.where(pattern_ref[stream, o] == b, 1, 0)
        hit = jnp.full(total.shape, found, jnp.int32) > 0
        total = total - jnp.where(hit, ref[0], 0.0)
    out_ref[...] = total


def per_device(pairs, narrow, rhs_panels, rhs_rest, diag_inv, couple, off_blocks, pattern, owner):
    _, rows, width = rhs_panels.shape
    depth = rows * narrow
    off_rows = off_blocks.shape[1]
    stack = rows + off_rows // 2
    chunks = (3 * rows + 2 * off_rows) // 2 // CH
    dma = pltpu.SemaphoreType.DMA
    vmem = pl.BlockSpec(memory_space=pltpu.VMEM)
    hbm = pl.BlockSpec(memory_space=pl.ANY)
    solved, updates = pl.pallas_call(
        functools.partial(panels_kernel, pairs, narrow),
        out_shape=(
            jax.ShapeDtypeStruct((2, rows, width), jnp.float32),
            jax.ShapeDtypeStruct((2, off_rows, width), jnp.float32),
        ),
        in_specs=[pl.BlockSpec(memory_space=pltpu.SMEM), vmem, hbm, hbm, hbm],
        out_specs=(vmem, vmem),
        scratch_shapes=[
            pltpu.VMEM((stack, depth), jnp.float32),
            pltpu.VMEM((stack, depth), jnp.float32),
            pltpu.VMEM((chunks, CH, depth), jnp.float32),
            pltpu.VMEM((chunks, CH, depth), jnp.float32),
            pltpu.VMEM((chunks, CH, depth), jnp.float32),
            pltpu.VMEM((4, depth, width), jnp.float32),
            pltpu.VMEM((2, depth, width), jnp.bfloat16),
            pltpu.VMEM((2, depth, width), jnp.bfloat16),
            dma((3,)),
            dma((3,)),
            dma((3,)),
            dma((chunks,)),
            dma((chunks,)),
            dma((chunks,)),
            dma((chunks,)),
            dma((chunks,)),
            dma((chunks,)),
            dma((4, narrow - 1)),
            dma((4, narrow - 1)),
        ],
        compiler_params=pltpu.CompilerParams(
            collective_id=0, has_side_effects=True, vmem_limit_bytes=60 * 2**20
        ),
        name="panels",
    )(owner, rhs_panels, diag_inv, couple, off_blocks)

    blocks = rhs_rest.shape[0] // BLK
    local = pattern - lax.axis_index("narrow") * blocks

    def place(stream):
        def index(b, pattern_ref):
            spot = jnp.int32(0)
            for o in range(pattern.shape[1]):
                spot = spot + jnp.where(pattern_ref[stream, o] == b, o, 0)
            return (stream, spot, 0)

        return index

    block = pl.BlockSpec((BLK, width), lambda b, pattern_ref: (b, 0))
    rest_out = pl.pallas_call(
        subtract_kernel,
        out_shape=jax.ShapeDtypeStruct(rhs_rest.shape, jnp.float32),
        grid_spec=pltpu.PrefetchScalarGridSpec(
            num_scalar_prefetch=1,
            grid=(blocks,),
            in_specs=[
                block,
                pl.BlockSpec((1, BLK, width), place(0)),
                pl.BlockSpec((1, BLK, width), place(1)),
            ],
            out_specs=block,
        ),
        name="subtract",
    )(local, rhs_rest, updates, updates)
    return solved, rest_out


def solution(mesh):
    in_specs = (
        P(None, "narrow", "wide"),
        P("narrow", "wide"),
        P("wide", "narrow", None),
        P("wide", "narrow", None),
        P("wide", "narrow", None),
        P(None, "narrow"),
        P(),
    )
    out_specs = (P(None, "narrow", "wide"), P("narrow", "wide"))
    step = functools.partial(per_device, mesh.shape["wide"] // 2, mesh.shape["narrow"])
    return jax.shard_map(
        step, mesh=mesh, in_specs=in_specs, out_specs=out_specs, check_vma=False
    )
```

time: 517 us -> 213 us (0.41)
  waiting for transfers between devices: 399 us -> 0 us
  Pallas kernels: 0 us -> 211 us
  matrix products: 58.2 us -> 0 us
  other arithmetic: 22.7 us -> 1.24 us
  between operations: 16.8 us -> 0.65 us
  local copies, waits for them, and re-layouts: 15.9 us -> 0.97 us
    psum x1 -> x0, waiting for transfers between devices: 295 us -> none  [from_root(): return lax.psum(block, axis)]
    pallas_call x0 -> x2, Pallas kernels: none -> 211 us  [the longest x1 198 us: per_device(): pl.pallas_call(functools.partial(panels_kernel, pairs, narrow), out_shape...]
    all_gather x4 -> x0, waiting for transfers between devices: 105 us -> none  [the longest x2 58.7 us: solve_panel(): full_rhs = lax.all_gather(rows_here, 'narrow', axis=0, tiled=True)]
    dot_general x7 -> x0, matrix products: 58.2 us -> none  [the longest x5 47.6 us: matmul(): jnp.dot(left, right, preferred_element_type=jnp.float32, precision=lax.Pr...]
    select_n x2 -> x0, other arithmetic: 12.8 us -> none  [from_root(): jnp.where(lax.axis_index(axis) == owner, block, jnp.zeros_like(block))]
    dot_general x2 -> x0, local copies, waits for them, and re-layouts: 12.6 us -> none  [apply_panel(): jnp.einsum('ob,orc->brc', select, updates, precision=lax.Precision.HIGHEST)]
    sub x2 -> x1, other arithmetic: 8.92 us -> 1.24 us  [per_device(): local = pattern - lax.axis_index('narrow') * blocks]
  transfers between devices with their start and end apart: 5 -> 0, of which waited for: 5 -> 0; matrix products, arithmetic and copies ran while one was open for 8% -> 0% of each run, Pallas kernels for 0% -> 0%
where the time goes in v1:
time: 213 us
  Pallas kernels  211 us (99%)
    pallas_call x1, Pallas kernels, per_device(): pl.pallas_call(functools.partial(panels_kernel, pairs, narrow), out_shape...  198 us
    pallas_call x1, Pallas kernels, per_device(): pl.pallas_call(subtract_kernel, out_shape=jax.ShapeDtypeStruct(rhs_rest.s...  13 us

profile of v1, /device:TPU:0, one launch (start us, length us, event | category | flops | bytes accessed | tf_op | source)
XLA Modules:
  0.0 213.4 jit_solution(8157730838194024269)
XLA Ops:
  0.6 1.2 broadcast_subtract_fusion.pattern_ref
  1.9 197.5 %panels.1 = (f32[2,256,512]{2,1,0:T(8,128)}, f32[2,1536,512]{2,1,0:T(8,128)}) custom-call(s32[2]{0:T(128)} %owner_ref.1, f32[2,256,512]{2,1,0:T(8,128)} %rhs_ref.1, f32[1,256,1024]{2,1,0:T(8,128)} %diag_ref.1, f32[1,256,1024]{2,1,0:T(8,128)} %couple_ref.1, f32[1,1536,1024]{2,1,0:T(8,128)} %off_ref.1), custom_call_target="tpu_custom_call" | custom-call | tf_op jit(solution)/shard_map/panels/pallas_call | solution.py:298
  199.4 0.0 copy-start
  199.4 13.0 %subtract.1 = f32[3072,512]{1,0:T(8,128)} custom-call(s32[2,6]{1,0:T(2,128)} %broadcast_subtract_fusion.pattern_ref, f32[3072,512]{1,0:T(8,128)} %rest_ref.1, f32[2,1536,512]{2,1,0:T(8,128)} %get-tuple-element.5.first_ref.second_ref, f32[2,1536,512]{2,1,0:T(8,128)} %get-tuple-element.5.first_ref.second_ref), custom_call_target="tpu_custom_call" | custom-call | tf_op jit(solution)/shard_map/subtract/pallas_call | solution.py:346
  212.4 0.0 copy-done
  212.4 1.0 copy.10
Async XLA Ops:
  199.4 13.0 %copy-start = (f32[2,256,512]{2,1,0:T(8,128)S(1)}, f32[2,256,512]{2,1,0:T(8,128)}, u32[]{:S(2)}) copy-start(f32[2,256,512]{2,1,0:T(8,128)} %get-tuple-element.8) | copy-start | bytes 3145732

commit v2 on v1

--- a/solution.py
+++ b/solution.py
@@ -9,7 +9,7 @@
 
 BLK = 256
 CH = 32
-SKEW = 2
+SKEW = 4
 GROUP = 4
 GAP = 10
 
@@ -214,7 +214,7 @@
         far = dot3(other[pl.ds(first, GROUP)].reshape(size, depth), xh[stream], xl[stream])
         u_ref[stream, pl.ds((1 - half) * off_part + group * size, size)] = far
 
-    lag = SKEW * pairs
+    lag = SKEW * (pairs - 1) + 1
     first_at = max(3 * nd + GROUP, nd + GAP + 1)
     second_at = 3 * nd + no + GROUP
 
@@ -337,8 +337,8 @@
         def index(b, pattern_ref):
             spot = jnp.int32(0)
             for o in range(pattern.shape[1]):
-                spot = spot + jnp.where(pattern_ref[stream, o] == b, o, 0)
-            return (stream, spot, 0)
+                spot = spot + jnp.where(pattern_ref[stream, o] <= b, 1, 0)
+            return (stream, jnp.maximum(spot - 1, 0), 0)
 
         return index
 

time: 213 us -> 218 us (1.023)
  Pallas kernels: 211 us -> 215 us
    pallas_call x1, Pallas kernels: 198 us -> 203 us  [per_device(): pl.pallas_call(functools.partial(panels_kernel, pairs, narrow), out_shape...]
where the time goes in v2:
time: 218 us; the launch traced here: 217 us
  Pallas kernels  215 us (99%)
    pallas_call x1, Pallas kernels, per_device(): pl.pallas_call(functools.partial(panels_kernel, pairs, narrow), out_shape...  203 us
    pallas_call x1, Pallas kernels, per_device(): pl.pallas_call(subtract_kernel, out_shape=jax.ShapeDtypeStruct(rhs_rest.s...  11.6 us

profile of v2, /device:TPU:0, one launch (start us, length us, event | category | flops | bytes accessed | tf_op | source)
XLA Modules:
  0.0 217.4 jit_solution(7930647625837258875)
XLA Ops:
  0.6 1.2 broadcast_subtract_fusion.pattern_ref
  1.9 203.0 %panels.1 = (f32[2,256,512]{2,1,0:T(8,128)}, f32[2,1536,512]{2,1,0:T(8,128)}) custom-call(s32[2]{0:T(128)} %owner_ref.1, f32[2,256,512]{2,1,0:T(8,128)} %rhs_ref.1, f32[1,256,1024]{2,1,0:T(8,128)} %diag_ref.1, f32[1,256,1024]{2,1,0:T(8,128)} %couple_ref.1, f32[1,1536,1024]{2,1,0:T(8,128)} %off_ref.1), custom_call_target="tpu_custom_call" | custom-call | tf_op jit(solution)/shard_map/panels/pallas_call | solution.py:298
  204.8 0.0 copy-start
  204.9 11.6 %subtract.1 = f32[3072,512]{1,0:T(8,128)} custom-call(s32[2,6]{1,0:T(2,128)} %broadcast_subtract_fusion.pattern_ref, f32[3072,512]{1,0:T(8,128)} %rest_ref.1, f32[2,1536,512]{2,1,0:T(8,128)} %get-tuple-element.5.first_ref.second_ref, f32[2,1536,512]{2,1,0:T(8,128)} %get-tuple-element.5.first_ref.second_ref), custom_call_target="tpu_custom_call" | custom-call | tf_op jit(solution)/shard_map/subtract/pallas_call | solution.py:346
  216.4 0.0 copy-done
  216.4 1.0 copy.10
Async XLA Ops:
  204.8 11.6 %copy-start = (f32[2,256,512]{2,1,0:T(8,128)S(1)}, f32[2,256,512]{2,1,0:T(8,128)}, u32[]{:S(2)}) copy-start(f32[2,256,512]{2,1,0:T(8,128)} %get-tuple-element.8) | copy-start | bytes 3145732

commit v3 on v1

--- a/solution.py
+++ b/solution.py
@@ -9,7 +9,7 @@
 
 BLK = 256
 CH = 32
-SKEW = 2
+SKEW = 1
 GROUP = 4
 GAP = 10
 
@@ -214,7 +214,7 @@
         far = dot3(other[pl.ds(first, GROUP)].reshape(size, depth), xh[stream], xl[stream])
         u_ref[stream, pl.ds((1 - half) * off_part + group * size, size)] = far
 
-    lag = SKEW * pairs
+    lag = SKEW * (pairs - 1) + 2
     first_at = max(3 * nd + GROUP, nd + GAP + 1)
     second_at = 3 * nd + no + GROUP
 

time: 213 us -> 284 us (1.33)
  Pallas kernels: 211 us -> 281 us
    pallas_call x1, Pallas kernels: 198 us -> 268 us  [per_device(): pl.pallas_call(functools.partial(panels_kernel, pairs, narrow), out_shape...]
where the time goes in v3:
time: 284 us
  Pallas kernels  281 us (99%)
    pallas_call x1, Pallas kernels, per_device(): pl.pallas_call(functools.partial(panels_kernel, pairs, narrow), out_shape...  268 us
    pallas_call x1, Pallas kernels, per_device(): pl.pallas_call(subtract_kernel, out_shape=jax.ShapeDtypeStruct(rhs_rest.s...  12.7 us

profile of v3, /device:TPU:0, one launch (start us, length us, event | category | flops | bytes accessed | tf_op | source)
XLA Modules:
  0.0 283.8 jit_solution(5282446812363065805)
XLA Ops:
  0.6 1.2 broadcast_subtract_fusion.pattern_ref
  1.9 268.2 %panels.1 = (f32[2,256,512]{2,1,0:T(8,128)}, f32[2,1536,512]{2,1,0:T(8,128)}) custom-call(s32[2]{0:T(128)} %owner_ref.1, f32[2,256,512]{2,1,0:T(8,128)} %rhs_ref.1, f32[1,256,1024]{2,1,0:T(8,128)} %diag_ref.1, f32[1,256,1024]{2,1,0:T(8,128)} %couple_ref.1, f32[1,1536,1024]{2,1,0:T(8,128)} %off_ref.1), custom_call_target="tpu_custom_call" | custom-call | tf_op jit(solution)/shard_map/panels/pallas_call | solution.py:298
  270.0 0.0 copy-start
  270.1 12.7 %subtract.1 = f32[3072,512]{1,0:T(8,128)} custom-call(s32[2,6]{1,0:T(2,128)} %broadcast_subtract_fusion.pattern_ref, f32[3072,512]{1,0:T(8,128)} %rest_ref.1, f32[2,1536,512]{2,1,0:T(8,128)} %get-tuple-element.5.first_ref.second_ref, f32[2,1536,512]{2,1,0:T(8,128)} %get-tuple-element.5.first_ref.second_ref), custom_call_target="tpu_custom_call" | custom-call | tf_op jit(solution)/shard_map/subtract/pallas_call | solution.py:346
  282.8 0.0 copy-done
  282.8 1.0 copy.10
Async XLA Ops:
  270.0 12.8 %copy-start = (f32[2,256,512]{2,1,0:T(8,128)S(1)}, f32[2,256,512]{2,1,0:T(8,128)}, u32[]{:S(2)}) copy-start(f32[2,256,512]{2,1,0:T(8,128)} %get-tuple-element.8) | copy-start | bytes 3145732
